TPU v7x, 32 devices: a whole 2x2x4 slice. The times are simulated.
32 devices in a mesh: band: 4 (over x, core), span: 8 (over z, y).
Axes of the slice: x: 2, y: 2, z: 4, core: 2. Of those that a mesh axis runs over, the one named last changes fastest.
Arguments:
- gases: bfloat16 [7, 32, 16384], P(None, None, ('band', 'span')), may hold values from 0 to 1
- pressure_bin: int32 [32, 16384], P(None, ('band', 'span')), may hold values from 0 to 59
- layer_mass: bfloat16 [32, 16384], P(None, ('band', 'span')), may hold values from 0.5 to 2
- cos_zenith: bfloat16 [16384], P(('band', 'span')), may hold values from 0.19921875 to 1
- surface_albedo: bfloat16 [16384], P(('band', 'span')), may hold values from 0.049804688 to 0.8984375
- column_order: int32 [16384], P(('band', 'span')), may hold values from 0 to 511, as said below
- sunlit: int32 [128], P(('band', 'span')), may hold values from 0 to 1, as said below
- absorption: bfloat16 [112, 7, 60], replicated, may hold values from 9.9658966e-05 to 0.099609375
- scattering: bfloat16 [112, 60], replicated, may hold values from 0.19921875 to 0.94921875
Outputs:
- heating: float32 [32, 16384], P(None, ('band', 'span'))
Inputs may be any that keep to these rules, and one draw needn't show every extreme that they name: `column_order`: the 512 entries of each device's slice are a permutation of 0 to 511. The 4 devices with the same index along the second mesh axis hold 8 sunlit blocks together; among them one device has all 4 blocks sunlit and one has none.
All inputs are finite; a program needn't handle non-finite values.
Results may differ from a plain program's by a relative error of at most 0.0003.
Values may be sent and summed in bfloat16 or wider, within the bound.
No kernel may reach another device: no remote copies, remote signals or barrier semaphores. Data moves between devices by JAX's collectives and lax.ppermute only.
A program may use at most 64 MiB of HBM per device.

v0:
```python
import functools
import math

import jax
import jax.numpy as jnp
from jax import lax
from jax.experimental import pallas as pl
from jax.experimental.pallas import tpu as pltpu
from jax.sharding import PartitionSpec as P

LANES = 128
ROWS = 8
PACK = 16
STEP = 4
HALVES = 2
BIN_ROWS = 64
LOG2E = math.log2(math.e)
VMEM_BYTES = 63 * 1024 * 1024


def one_hot(hit):
    return jnp.where(hit, 1.0, 0.0).astype(jnp.bfloat16)


def heating_kernel(
    per_peer,
    gases_hbm,
    bins_hbm,
    mass_hbm,
    cosine_hbm,
    ground_hbm,
    order_hbm,
    absorb_hbm,
    scatter_hbm,
    heat_ref,
    owner_ref,
    gases_ref,
    bins_ref,
    mass_ref,
    cosine_ref,
    ground_ref,
    order_ref,
    absorb_ref,
    albedo_ref,
    copied,
    wide_buf,
    table_ref,
    scatter_ref,
    block_ref,
    optic_ref,
    up_buf,
    rise_buf,
    pass_buf,
    refl_buf,
    fall_buf,
    direct_buf,
    gain_buf,
    net_buf,
    warm_ref,
):
    gas_count, levels, columns = gases_ref.shape
    points = table_ref.shape[0]
    bin_count = absorb_ref.shape[1]
    half = points // HALVES
    vregs = half // ROWS
    blocks = columns // LANES
    bin_row = gas_count * levels
    ray_row = bin_row + levels
    first_row = gas_count * BIN_ROWS

    copies = [
        pltpu.make_async_copy(source, target, copied.at[place])
        for place, (source, target) in enumerate(
            (
                (absorb_hbm, absorb_ref),
                (scatter_hbm, albedo_ref),
                (order_hbm, order_ref),
                (cosine_hbm, cosine_ref),
                (ground_hbm, ground_ref),
                (bins_hbm, bins_ref),
                (gases_hbm, gases_ref),
                (mass_hbm, mass_ref),
            )
        )
    ]
    for copy in copies:
        copy.start()

    wide_buf[...] = jnp.zeros_like(wide_buf)
    for copy in copies[:3]:
        copy.wait()

    square = (columns, columns)
    order = jnp.broadcast_to(order_ref[...], square)
    match = one_hot(order == lax.broadcasted_iota(jnp.int32, square, 0))
    place = lax.broadcasted_iota(jnp.int32, (ROWS, columns), 1)
    group = (place // per_peer).astype(jnp.float32).astype(jnp.bfloat16)
    owner_ref[...] = lax.dot_general(group, match, (((1,), (1,)), ((), ())), preferred_element_type=jnp.float32)

    for gas in range(gas_count):
        wide_buf[gas * BIN_ROWS : gas * BIN_ROWS + bin_count, :points] = absorb_ref[gas].astype(jnp.float32)
    wide_buf[first_row : first_row + bin_count, :points] = 0.5 * albedo_ref[...].astype(jnp.float32)
    turned = [
        jnp.transpose(wide_buf[i * LANES : (i + 1) * LANES])[:points].astype(jnp.bfloat16)
        for i in range(wide_buf.shape[0] // LANES)
    ]
    whole = jnp.concatenate(turned, axis=1)
    table_ref[...] = whole[:, :first_row]
    scatter_ref[...] = whole[:, first_row : first_row + BIN_ROWS]
    for copy in copies[3:]:
        copy.wait()

    for block in range(blocks):
        cols = slice(block * LANES, (block + 1) * LANES)
        for gas in range(gas_count):
            block_ref[block, gas * levels : (gas + 1) * levels] = gases_ref[gas, :, cols].astype(jnp.float32)
        block_ref[block, bin_row:ray_row] = bins_ref[:, cols].astype(jnp.float32)
    wide = (1, columns)
    cosines = cosine_ref[...].astype(jnp.float32).reshape(wide)
    grounds = ground_ref[...].astype(jnp.float32).reshape(wide)
    for block in range(blocks):
        cols = slice(block * LANES, (block + 1) * LANES)
        block_ref[block, ray_row : ray_row + ROWS] = jnp.broadcast_to(cosines[:, cols], (ROWS, LANES))
        block_ref[block, ray_row + ROWS : ray_row + 2 * ROWS] = jnp.broadcast_to(grounds[:, cols], (ROWS, LANES))

    def optical(slot, layer):
        parts = []
        shape = (BIN_ROWS, LANES)
        rows = lax.broadcasted_iota(jnp.int32, shape, 0).astype(jnp.float32)
        selectors = []
        for near in (layer, layer + 1):
            place = bin_row + near
            bins = jnp.broadcast_to(block_ref[slot, place : place + 1, :], shape)
            selectors.append(one_hot(bins == rows))
        for gas in range(gas_count):
            pair = []
            for near, selector in zip((layer, layer + 1), selectors):
                place = gas * levels + near
                amount = jnp.broadcast_to(block_ref[slot, place : place + 1, :], (PACK, LANES)).astype(jnp.bfloat16)
                pair.append(jnp.concatenate([amount] * (BIN_ROWS // PACK), axis=0) * selector)
            parts.append(jnp.concatenate(pair, axis=1))
        weighted = jnp.concatenate(parts, axis=0)
        selected = jnp.concatenate(selectors, axis=1)
        tau = jnp.dot(table_ref[...], weighted, preferred_element_type=jnp.float32)
        albedo = jnp.dot(scatter_ref[...], selected, preferred_element_type=jnp.float32)
        for near in range(2):
            cols = slice(near * LANES, (near + 1) * LANES)
            optic_ref[layer + near, :points] = tau[:, cols]
            optic_ref[layer + near, points:] = albedo[:, cols]

    def advance(first, part, slope):
        rows = slice(part * half, (part + 1) * half)
        half_rows = slice(points + part * half, points + (part + 1) * half)
        shape = (vregs, ROWS, LANES)
        refl = refl_buf[rows].reshape(shape)
        fall = fall_buf[rows].reshape(shape)
        direct = direct_buf[rows].reshape(shape)
        for layer in range(first, first + STEP):
            tau = optic_ref[layer, rows].reshape(shape)
            half_albedo = optic_ref[layer, half_rows].reshape(shape)
            fading = jnp.exp2(tau * (-1.66 * LOG2E))
            passed = jnp.exp2(tau * slope)
            reflect = half_albedo * (1.0 - fading)
            transmit = fading + reflect
            below = direct * passed
            source = half_albedo * (direct - below)
            pass_buf[layer, rows] = (1.0 - refl).reshape(half, LANES)
            inverse = pl.reciprocal(1.0 - reflect * refl, approx=True)
            up = transmit * inverse
            rise = (reflect * fall + source) * inverse
            up_buf[layer, rows] = up.reshape(half, LANES)
            rise_buf[layer, rows] = rise.reshape(half, LANES)
            fall = source + transmit * (fall + refl * rise)
            refl = reflect + transmit * (refl * up)
            direct = below
            gain_buf[part, layer + 1] = jnp.sum(direct + fall, axis=0)
        refl_buf[rows] = refl.reshape(half, LANES)
        fall_buf[rows] = fall.reshape(half, LANES)
        direct_buf[rows] = direct.reshape(half, LANES)

    lead = range(0, STEP, 2)

    def column_block(block, carry):
        cosine = block_ref[block, ray_row : ray_row + ROWS]
        slope = (-LOG2E) / cosine
        refl_buf[...] = jnp.zeros_like(refl_buf)
        fall_buf[...] = jnp.zeros_like(fall_buf)
        direct_buf[...] = jnp.broadcast_to(cosine[:1], direct_buf.shape)
        for part in range(HALVES):
            gain_buf[part, 0] = cosine * float(vregs)
        for first in range(0, levels, STEP):
            coming = [layer for layer in range(first + STEP, first + 2 * STEP, 2) if layer < levels]
            for part in range(HALVES):
                for layer in coming[part * len(coming) // HALVES : (part + 1) * len(coming) // HALVES]:
                    optical(block, layer)
                advance(first, part, slope)

        following = jnp.minimum(block + 1, blocks - 1)
        for layer in lead:
            optical(following, layer)

        albedo = block_ref[block, ray_row + ROWS : ray_row + 2 * ROWS]
        shape = (points // ROWS, ROWS, LANES)
        refl = refl_buf[...].reshape(shape)
        arriving = (fall_buf[...] + direct_buf[...]).reshape(shape)
        rising = albedo * arriving * pl.reciprocal(1.0 - albedo * refl, approx=True)

        def total(level):
            summed = gain_buf[0, level]
            for part in range(1, HALVES):
                summed = summed + gain_buf[part, level]
            return summed

        net_buf[levels] = total(levels) - jnp.sum(rising * (1.0 - refl), axis=0)
        for layer in range(levels - 1, -1, -1):
            rising = up_buf[layer].reshape(shape) * rising + rise_buf[layer].reshape(shape)
            net_buf[layer] = total(layer) - jnp.sum(rising * pass_buf[layer].reshape(shape), axis=0)
        warm_ref[block] = jnp.sum(net_buf[:levels] - net_buf[1:], axis=1)
        return carry

    for layer in lead:
        optical(0, layer)
    lax.fori_loop(0, blocks, column_block, 0)

    for block in range(blocks):
        cols = slice(block * LANES, (block + 1) * LANES)
        heat_ref[:, cols] = warm_ref[block] / mass_ref[:, cols].astype(jnp.float32)


def shade_kernel(heat_hbm, owner_hbm, flags_hbm, out_ref, heat_ref, owner_ref, flags_ref, copied):
    copies = [
        pltpu.make_async_copy(source, target, copied.at[place])
        for place, (source, target) in enumerate(
            ((heat_hbm, heat_ref), (owner_hbm, owner_ref), (flags_hbm, flags_ref))
        )
    ]
    for copy in copies:
        copy.start()
    for copy in copies:
        copy.wait()
    owner = owner_ref[...]
    lit = jnp.zeros_like(owner)
    for group in range(flags_ref.shape[0]):
        flag = jnp.broadcast_to(flags_ref[group].astype(jnp.float32), owner.shape)
        lit = jnp.where(owner == float(group), flag, lit)
    out_ref[...] = heat_ref[...] * lit[:1]


def local(
    gases,
    pressure_bin,
    layer_mass,
    cos_zenith,
    surface_albedo,
    column_order,
    sunlit,
    absorption,
    scattering,
):
    group_size = lax.axis_size("span")
    gas_count, levels, columns = gases.shape
    points, _, bins = absorption.shape
    block_count = sunlit.shape[0]
    wanted = jnp.broadcast_to(sunlit[:, None], (block_count, group_size // block_count)).reshape(group_size, 1, 1)
    flags = lax.all_to_all(wanted, "span", split_axis=0, concat_axis=0, tiled=True)
    field = pltpu.VMEM((levels, points, LANES), jnp.float32)
    state = pltpu.VMEM((points, LANES), jnp.float32)
    rows = gas_count * levels + levels + PACK
    blocks = columns // LANES
    heat, owner = pl.pallas_call(
        functools.partial(heating_kernel, columns // group_size),
        out_shape=(
            jax.ShapeDtypeStruct((levels, columns), jnp.float32),
            jax.ShapeDtypeStruct((ROWS, columns), jnp.float32),
        ),
        in_specs=[pl.BlockSpec(memory_space=pltpu.HBM)] * 8,
        out_specs=(pl.BlockSpec(memory_space=pltpu.VMEM),) * 2,
        scratch_shapes=[
            pltpu.VMEM(gases.shape, gases.dtype),
            pltpu.VMEM(pressure_bin.shape, pressure_bin.dtype),
            pltpu.VMEM(layer_mass.shape, layer_mass.dtype),
            pltpu.VMEM(cos_zenith.shape, cos_zenith.dtype),
            pltpu.VMEM(surface_albedo.shape, surface_albedo.dtype),
            pltpu.VMEM((1, columns), column_order.dtype),
            pltpu.VMEM((gas_count, bins, points), absorption.dtype),
            pltpu.VMEM((bins, points), scattering.dtype),
            pltpu.SemaphoreType.DMA((8,)),
            pltpu.VMEM((-(-(gas_count + 1) * BIN_ROWS // LANES) * LANES, LANES), jnp.float32),
            pltpu.VMEM((points, gas_count * BIN_ROWS), jnp.bfloat16),
            pltpu.VMEM((points, BIN_ROWS), jnp.bfloat16),
            pltpu.VMEM((blocks, rows, LANES), jnp.float32),
            pltpu.VMEM((levels, 2 * points, LANES), jnp.float32),
            field,
            field,
            field,
            state,
            state,
            state,
            pltpu.VMEM((HALVES, levels + 1, ROWS, LANES), jnp.float32),
            pltpu.VMEM((levels + 1, ROWS, LANES), jnp.float32),
            pltpu.VMEM((blocks, levels, LANES), jnp.float32),
        ],
        compiler_params=pltpu.CompilerParams(vmem_limit_bytes=VMEM_BYTES),
        cost_estimate=pl.CostEstimate(
            flops=40 * levels * points * columns, bytes_accessed=1 << 20, transcendentals=3 * levels * points * columns
        ),
    )(
        gases,
        pressure_bin,
        layer_mass,
        cos_zenith,
        surface_albedo,
        column_order.reshape(1, columns),
        jnp.transpose(absorption, (1, 2, 0)),
        jnp.transpose(scattering),
    )
    return pl.pallas_call(
        shade_kernel,
        out_shape=jax.ShapeDtypeStruct(heat.shape, heat.dtype),
        in_specs=[pl.BlockSpec(memory_space=pltpu.HBM)] * 3,
        out_specs=pl.BlockSpec(memory_space=pltpu.VMEM),
        scratch_shapes=[
            pltpu.VMEM(heat.shape, heat.dtype),
            pltpu.VMEM(owner.shape, owner.dtype),
            pltpu.VMEM(flags.shape, flags.dtype),
            pltpu.SemaphoreType.DMA((3,)),
        ],
        compiler_params=pltpu.CompilerParams(vmem_limit_bytes=VMEM_BYTES),
    )(heat, owner, flags)


def solution(mesh):
    placed = (
        P(None, None, ("band", "span")),
        P(None, ("band", "span")),
        P(None, ("band", "span")),
        P(("band", "span")),
        P(("band", "span")),
        P(("band", "span")),
        P(("band", "span")),
        P(),
        P(),
    )
    return jax.shard_map(
        local, mesh=mesh, in_specs=placed, out_specs=P(None, ("band", "span")), check_vma=False
    )
```

profile of v0, /device:TPU:0, one launch (start us, length us, event | category | flops | bytes accessed | tf_op | source)
XLA Modules:
  0.0 23.1 jit_solution(9252700483665280415)
XLA Ops:
  0.0 0.7 %broadcast_in_dim.2 = s32[4,2]{1,0:T(4,128)S(1)} broadcast(s32[4]{0:T(128)} %param.15), dimensions={0} | broadcast | bytes 48 | tf_op jit(solution)/shard_map/broadcast_in_dim | solution.py:264
  0.7 0.7 %reshape.9 = s32[8,1,1]{2,1,0:T(1,128)} reshape(s32[4,2]{1,0:T(4,128)S(1)} %broadcast_in_dim.2) | data formatting | bytes 64 | tf_op jit(solution)/shard_map/reshape | solution.py:264
  1.4 7.3 %all-to-all-start = ((s32[8,1,1]{2,1,0:T(1,128)}), s32[8,1,1]{2,1,0:T(1,128)S(1)}, u32[]{:S(2)}, u32[]{:S(2)}) async-start(s32[8,1,1]{2,1,0:T(1,128)} %reshape.9), calls=%async_computation | async-start | bytes 8192 | tf_op jit(solution)/shard_map/all_to_all | solution.py:265
  8.7 12.2 %shard_map.91 = (f32[32,512]{1,0:T(8,128)}, f32[8,512]{1,0:T(8,128)}) custom-call(bf16[7,32,512]{2,1,0:T(8,128)(2,1)} %gases_hbm.1, s32[32,512]{1,0:T(8,128)} %bins_hbm.1, bf16[32,512]{1,0:T(8,128)(2,1)} %mass_hbm.1, bf16[512]{0:T(512)(128)(2,1)} %cosine_hbm.1, bf16[512]{0:T(512)(128)(2,1)} %ground_hbm.1, s32[1,512]{1,0:T(1,128)} %bitcast.5, ...), custom_call_target="tpu_custom_call" | custom-call | flops 73400320 | bytes 1048576 | tf_op jit(solution)/shard_map/pallas_call | solution.py:270
  20.9 0.0 all-to-all-done.flags_hbm
  20.9 0.0 copy-start
  20.9 0.6 %copy-done = s32[8,1,1]{2,1,0:T(1,128)} copy-done((s32[8,1,1]{2,1,0:T(1,128)}, s32[8,1,1]{2,1,0:T(1,128)S(1)}, u32[]{:S(2)}) %copy-start) | copy-done | bytes 56
  21.5 1.6 %shard_map.92 = f32[32,512]{1,0:T(8,128)} custom-call(f32[32,512]{1,0:T(8,128)} %get-tuple-element.7.heat_hbm, f32[8,512]{1,0:T(8,128)} %get-tuple-element.8.owner_hbm, s32[8,1,1]{2,1,0:T(1,128)} %copy-done), custom_call_target="tpu_custom_call" | custom-call | tf_op jit(solution)/shard_map/pallas_call | solution.py:317
Async XLA Ops:
  1.4 19.5 %all-to-all-start = ((s32[8,1,1]{2,1,0:T(1,128)}), s32[8,1,1]{2,1,0:T(1,128)S(1)}, u32[]{:S(2)}, u32[]{:S(2)}) async-start(s32[8,1,1]{2,1,0:T(1,128)} %reshape.9), calls=%async_computation | async-start | bytes 8192 | tf_op jit(solution)/shard_map/all_to_all | solution.py:265
  20.9 0.6 %copy-start = (s32[8,1,1]{2,1,0:T(1,128)}, s32[8,1,1]{2,1,0:T(1,128)S(1)}, u32[]{:S(2)}) copy-start(s32[8,1,1]{2,1,0:T(1,128)S(1)} %all-to-all-done.flags_hbm) | copy-start | bytes 100
where the time goes:
time: 23.3 us; the launch traced here: 23.1 us
  Pallas kernels  13.8 us (59%)
  starting transfers between devices  7.28 us (31%)
  local copies, waits for them, and re-layouts  1.99 us (9%)
    pallas_call x1, Pallas kernels, local(): pl.pallas_call(functools.partial(heating_kernel, columns // group_size),...  12.2 us
    all_to_all x1, starting transfers between devices, local(): lax.all_to_all(wanted, 'span', split_axis=0, concat_axis=0, tiled=True)  7.28 us
    pallas_call x1, Pallas kernels, local(): pl.pallas_call(shade_kernel, out_shape=jax.ShapeDtypeStruct(heat.shape, h...  1.58 us
    broadcast_in_dim x1, local copies, waits for them, and re-layouts, local(): jnp.broadcast_to(sunlit[:, None], (block_count, group_size // block_count))  0.72 us
    reshape x1, local copies, waits for them, and re-layouts, local(): jnp.broadcast_to(sunlit[:, None], (block_count, group_size // block_count))  0.68 us
    unnamed x2, local copies, waits for them, and re-layouts  0.59 us
  transfers between devices with their start and end apart: 1, of which 0 were waited for; matrix products, arithmetic and copies ran while one was open for 0% of the time, Pallas kernels for 53%

commit v1 on v0

--- a/solution.py
+++ b/solution.py
@@ -11,11 +11,12 @@
 LANES = 128
 ROWS = 8
 PACK = 16
-STEP = 4
+STEP = 8
 HALVES = 2
 BIN_ROWS = 64
 LOG2E = math.log2(math.e)
 VMEM_BYTES = 63 * 1024 * 1024
+SHADE_BYTES = 55200 * 1024
 
 
 def one_hot(hit):
@@ -33,7 +34,6 @@
     absorb_hbm,
     scatter_hbm,
     heat_ref,
-    owner_ref,
     gases_ref,
     bins_ref,
     mass_ref,
@@ -95,7 +95,7 @@
     match = one_hot(order == lax.broadcasted_iota(jnp.int32, square, 0))
     place = lax.broadcasted_iota(jnp.int32, (ROWS, columns), 1)
     group = (place // per_peer).astype(jnp.float32).astype(jnp.bfloat16)
-    owner_ref[...] = lax.dot_general(group, match, (((1,), (1,)), ((), ())), preferred_element_type=jnp.float32)
+    heat_ref[levels:] = lax.dot_general(group, match, (((1,), (1,)), ((), ())), preferred_element_type=jnp.float32)
 
     for gas in range(gas_count):
         wide_buf[gas * BIN_ROWS : gas * BIN_ROWS + bin_count, :points] = absorb_ref[gas].astype(jnp.float32)
@@ -126,12 +126,15 @@
     def optical(slot, layer):
         parts = []
         shape = (BIN_ROWS, LANES)
-        rows = lax.broadcasted_iota(jnp.int32, shape, 0).astype(jnp.float32)
+        rows = lax.broadcasted_iota(jnp.int32, shape, 0).astype(jnp.float32).astype(jnp.bfloat16)
+        one = jnp.ones(shape, jnp.bfloat16)
+        zero = jnp.zeros(shape, jnp.bfloat16)
         selectors = []
         for near in (layer, layer + 1):
             place = bin_row + near
-            bins = jnp.broadcast_to(block_ref[slot, place : place + 1, :], shape)
-            selectors.append(one_hot(bins == rows))
+            bins = jnp.broadcast_to(block_ref[slot, place : place + 1, :], (PACK, LANES)).astype(jnp.bfloat16)
+            bins = jnp.concatenate([bins] * (BIN_ROWS // PACK), axis=0)
+            selectors.append(jnp.where(bins == rows, one, zero))
         for gas in range(gas_count):
             pair = []
             for near, selector in zip((layer, layer + 1), selectors):
@@ -148,13 +151,16 @@
             optic_ref[layer + near, :points] = tau[:, cols]
             optic_ref[layer + near, points:] = albedo[:, cols]
 
-    def advance(first, part, slope):
+    def advance(first, part, cosine, slope):
         rows = slice(part * half, (part + 1) * half)
         half_rows = slice(points + part * half, points + (part + 1) * half)
         shape = (vregs, ROWS, LANES)
-        refl = refl_buf[rows].reshape(shape)
-        fall = fall_buf[rows].reshape(shape)
-        direct = direct_buf[rows].reshape(shape)
+        if first > 0:
+            refl = refl_buf[rows].reshape(shape)
+            fall = fall_buf[rows].reshape(shape)
+            direct = direct_buf[rows].reshape(shape)
+        else:
+            direct = jnp.broadcast_to(cosine[None], shape)
         for layer in range(first, first + STEP):
             tau = optic_ref[layer, rows].reshape(shape)
             half_albedo = optic_ref[layer, half_rows].reshape(shape)
@@ -164,14 +170,20 @@
             transmit = fading + reflect
             below = direct * passed
             source = half_albedo * (direct - below)
-            pass_buf[layer, rows] = (1.0 - refl).reshape(half, LANES)
-            inverse = pl.reciprocal(1.0 - reflect * refl, approx=True)
-            up = transmit * inverse
-            rise = (reflect * fall + source) * inverse
-            up_buf[layer, rows] = up.reshape(half, LANES)
-            rise_buf[layer, rows] = rise.reshape(half, LANES)
-            fall = source + transmit * (fall + refl * rise)
-            refl = reflect + transmit * (refl * up)
+            if layer == 0:
+                up_buf[layer, rows] = transmit.reshape(half, LANES)
+                rise_buf[layer, rows] = source.reshape(half, LANES)
+                fall = source
+                refl = reflect
+            else:
+                pass_buf[layer, rows] = (1.0 - refl).reshape(half, LANES)
+                inverse = pl.reciprocal(1.0 - reflect * refl, approx=True)
+                up = transmit * inverse
+                rise = (reflect * fall + source) * inverse
+                up_buf[layer, rows] = up.reshape(half, LANES)
+                rise_buf[layer, rows] = rise.reshape(half, LANES)
+                fall = source + transmit * (fall + refl * rise)
+                refl = reflect + transmit * (refl * up)
             direct = below
             gain_buf[part, layer + 1] = jnp.sum(direct + fall, axis=0)
         refl_buf[rows] = refl.reshape(half, LANES)
@@ -183,9 +195,6 @@
     def column_block(block, carry):
         cosine = block_ref[block, ray_row : ray_row + ROWS]
         slope = (-LOG2E) / cosine
-        refl_buf[...] = jnp.zeros_like(refl_buf)
-        fall_buf[...] = jnp.zeros_like(fall_buf)
-        direct_buf[...] = jnp.broadcast_to(cosine[:1], direct_buf.shape)
         for part in range(HALVES):
             gain_buf[part, 0] = cosine * float(vregs)
         for first in range(0, levels, STEP):
@@ -193,7 +202,7 @@
             for part in range(HALVES):
                 for layer in coming[part * len(coming) // HALVES : (part + 1) * len(coming) // HALVES]:
                     optical(block, layer)
-                advance(first, part, slope)
+                advance(first, part, cosine, slope)
 
         following = jnp.minimum(block + 1, blocks - 1)
         for layer in lead:
@@ -214,7 +223,8 @@
         net_buf[levels] = total(levels) - jnp.sum(rising * (1.0 - refl), axis=0)
         for layer in range(levels - 1, -1, -1):
             rising = up_buf[layer].reshape(shape) * rising + rise_buf[layer].reshape(shape)
-            net_buf[layer] = total(layer) - jnp.sum(rising * pass_buf[layer].reshape(shape), axis=0)
+            taken = rising if layer == 0 else rising * pass_buf[layer].reshape(shape)
+            net_buf[layer] = total(layer) - jnp.sum(taken, axis=0)
         warm_ref[block] = jnp.sum(net_buf[:levels] - net_buf[1:], axis=1)
         return carry
 
@@ -224,26 +234,20 @@
 
     for block in range(blocks):
         cols = slice(block * LANES, (block + 1) * LANES)
-        heat_ref[:, cols] = warm_ref[block] / mass_ref[:, cols].astype(jnp.float32)
-
-
-def shade_kernel(heat_hbm, owner_hbm, flags_hbm, out_ref, heat_ref, owner_ref, flags_ref, copied):
-    copies = [
-        pltpu.make_async_copy(source, target, copied.at[place])
-        for place, (source, target) in enumerate(
-            ((heat_hbm, heat_ref), (owner_hbm, owner_ref), (flags_hbm, flags_ref))
-        )
-    ]
-    for copy in copies:
-        copy.start()
-    for copy in copies:
-        copy.wait()
-    owner = owner_ref[...]
+        heat_ref[:levels, cols] = warm_ref[block] / mass_ref[:, cols].astype(jnp.float32)
+
+
+def shade_kernel(heat_hbm, flags_ref, out_ref, heat_ref, copied):
+    copy = pltpu.make_async_copy(heat_hbm, heat_ref, copied)
+    copy.start()
+    copy.wait()
+    levels = out_ref.shape[0]
+    owner = heat_ref[levels:]
     lit = jnp.zeros_like(owner)
     for group in range(flags_ref.shape[0]):
         flag = jnp.broadcast_to(flags_ref[group].astype(jnp.float32), owner.shape)
         lit = jnp.where(owner == float(group), flag, lit)
-    out_ref[...] = heat_ref[...] * lit[:1]
+    out_ref[...] = heat_ref[:levels] * lit[:1]
 
 
 def local(
@@ -267,14 +271,11 @@
     state = pltpu.VMEM((points, LANES), jnp.float32)
     rows = gas_count * levels + levels + PACK
     blocks = columns // LANES
-    heat, owner = pl.pallas_call(
+    heat = pl.pallas_call(
         functools.partial(heating_kernel, columns // group_size),
-        out_shape=(
-            jax.ShapeDtypeStruct((levels, columns), jnp.float32),
-            jax.ShapeDtypeStruct((ROWS, columns), jnp.float32),
-        ),
+        out_shape=jax.ShapeDtypeStruct((levels + ROWS, columns), jnp.float32),
         in_specs=[pl.BlockSpec(memory_space=pltpu.HBM)] * 8,
-        out_specs=(pl.BlockSpec(memory_space=pltpu.VMEM),) * 2,
+        out_specs=pl.BlockSpec(memory_space=pltpu.VMEM),
         scratch_shapes=[
             pltpu.VMEM(gases.shape, gases.dtype),
             pltpu.VMEM(pressure_bin.shape, pressure_bin.dtype),
@@ -316,17 +317,15 @@
     )
     return pl.pallas_call(
         shade_kernel,
-        out_shape=jax.ShapeDtypeStruct(heat.shape, heat.dtype),
-        in_specs=[pl.BlockSpec(memory_space=pltpu.HBM)] * 3,
+        out_shape=jax.ShapeDtypeStruct((levels, columns), heat.dtype),
+        in_specs=[pl.BlockSpec(memory_space=pltpu.HBM), pl.BlockSpec(memory_space=pltpu.VMEM)],
         out_specs=pl.BlockSpec(memory_space=pltpu.VMEM),
         scratch_shapes=[
             pltpu.VMEM(heat.shape, heat.dtype),
-            pltpu.VMEM(owner.shape, owner.dtype),
-            pltpu.VMEM(flags.shape, flags.dtype),
-            pltpu.SemaphoreType.DMA((3,)),
+            pltpu.SemaphoreType.DMA(()),
         ],
-        compiler_params=pltpu.CompilerParams(vmem_limit_bytes=VMEM_BYTES),
-    )(heat, owner, flags)
+        compiler_params=pltpu.CompilerParams(vmem_limit_bytes=SHADE_BYTES),
+    )(heat, flags)
 
 
 def solution(mesh):

time: 23.3 us -> 22.6 us (0.970)
  local copies, waits for them, and re-layouts: 1.99 us -> 1.4 us
    unnamed x2 -> x0, local copies, waits for them, and re-layouts: 0.59 us -> none
  transfers between devices with their start and end apart: 1 -> 1, of which waited for: 0 -> 0; matrix products, arithmetic and copies ran while one was open for 0% -> 0% of each run, Pallas kernels for 53% -> 54%
where the time goes in v1:
time: 22.6 us; the launch traced here: 22.4 us
  Pallas kernels  13.7 us (61%)
  starting transfers between devices  7.28 us (32%)
  local copies, waits for them, and re-layouts  1.4 us (6%)
    pallas_call x1, Pallas kernels, local(): pl.pallas_call(functools.partial(heating_kernel, columns // group_size),...  12 us
    all_to_all x1, starting transfers between devices, local(): lax.all_to_all(wanted, 'span', split_axis=0, concat_axis=0, tiled=True)  7.28 us
    pallas_call x1, Pallas kernels, local(): pl.pallas_call(shade_kernel, out_shape=jax.ShapeDtypeStruct((levels, colu...  1.61 us
    broadcast_in_dim x1, local copies, waits for them, and re-layouts, local(): jnp.broadcast_to(sunlit[:, None], (block_count, group_size // block_count))  0.72 us
    reshape x1, local copies, waits for them, and re-layouts, local(): jnp.broadcast_to(sunlit[:, None], (block_count, group_size // block_count))  0.68 us
  transfers between devices with their start and end apart: 1, of which 0 were waited for; matrix products, arithmetic and copies ran while one was open for 0% of the time, Pallas kernels for 54%

profile of v1, /device:TPU:0, one launch (start us, length us, event | category | flops | bytes accessed | tf_op | source)
XLA Modules:
  0.0 22.4 jit_solution(14297379523609107042)
XLA Ops:
  0.0 0.7 %broadcast_in_dim.2 = s32[4,2]{1,0:T(4,128)S(1)} broadcast(s32[4]{0:T(128)} %param.15), dimensions={0} | broadcast | bytes 48 | tf_op jit(solution)/shard_map/broadcast_in_dim | solution.py:268
  0.7 0.7 %reshape.9 = s32[8,1,1]{2,1,0:T(1,128)} reshape(s32[4,2]{1,0:T(4,128)S(1)} %broadcast_in_dim.2) | data formatting | bytes 64 | tf_op jit(solution)/shard_map/reshape | solution.py:268
  1.4 7.3 %all-to-all-start = ((s32[8,1,1]{2,1,0:T(1,128)}), s32[8,1,1]{2,1,0:T(1,128)S(1)}, u32[]{:S(2)}, u32[]{:S(2)}) async-start(s32[8,1,1]{2,1,0:T(1,128)} %reshape.9), calls=%async_computation | async-start | bytes 8192 | tf_op jit(solution)/shard_map/all_to_all | solution.py:269
  8.7 12.0 %shard_map.91.heat_hbm = f32[40,512]{1,0:T(8,128)} custom-call(bf16[7,32,512]{2,1,0:T(8,128)(2,1)} %gases_hbm.1, s32[32,512]{1,0:T(8,128)} %bins_hbm.1, bf16[32,512]{1,0:T(8,128)(2,1)} %mass_hbm.1, bf16[512]{0:T(512)(128)(2,1)} %cosine_hbm.1, bf16[512]{0:T(512)(128)(2,1)} %ground_hbm.1, s32[1,512]{1,0:T(1,128)} %bitcast.5, bf16[7,60,112]{2,1,0:T(8,128)(2,1)} %bitcast.3, ...), custom_call_target="tpu_custom_call" | custom-call | flops 73400320 | bytes 1048576 | tf_op jit(solution)/shard_map/pallas_call | solution.py:274
  20.7 0.0 all-to-all-done.flags_ref
  20.7 1.6 %shard_map.92 = f32[32,512]{1,0:T(8,128)} custom-call(f32[40,512]{1,0:T(8,128)} %shard_map.91.heat_hbm, s32[8,1,1]{2,1,0:T(1,128)S(1)} %all-to-all-done.flags_ref), custom_call_target="tpu_custom_call" | custom-call | tf_op jit(solution)/shard_map/pallas_call | solution.py:318
Async XLA Ops:
  1.4 19.3 %all-to-all-start = ((s32[8,1,1]{2,1,0:T(1,128)}), s32[8,1,1]{2,1,0:T(1,128)S(1)}, u32[]{:S(2)}, u32[]{:S(2)}) async-start(s32[8,1,1]{2,1,0:T(1,128)} %reshape.9), calls=%async_computation | async-start | bytes 8192 | tf_op jit(solution)/shard_map/all_to_all | solution.py:269

commit v2 on v1

--- a/solution.py
+++ b/solution.py
@@ -45,7 +45,7 @@
     copied,
     wide_buf,
     table_ref,
-    scatter_ref,
+    mixed_ref,
     block_ref,
     optic_ref,
     up_buf,
@@ -59,7 +59,7 @@
     warm_ref,
 ):
     gas_count, levels, columns = gases_ref.shape
-    points = table_ref.shape[0]
+    points, split = table_ref.shape
     bin_count = absorb_ref.shape[1]
     half = points // HALVES
     vregs = half // ROWS
@@ -101,12 +101,15 @@
         wide_buf[gas * BIN_ROWS : gas * BIN_ROWS + bin_count, :points] = absorb_ref[gas].astype(jnp.float32)
     wide_buf[first_row : first_row + bin_count, :points] = 0.5 * albedo_ref[...].astype(jnp.float32)
     turned = [
-        jnp.transpose(wide_buf[i * LANES : (i + 1) * LANES])[:points].astype(jnp.bfloat16)
+        jnp.transpose(wide_buf[i * LANES : (i + 1) * LANES])[:points]
         for i in range(wide_buf.shape[0] // LANES)
     ]
     whole = jnp.concatenate(turned, axis=1)
-    table_ref[...] = whole[:, :first_row]
-    scatter_ref[...] = whole[:, first_row : first_row + BIN_ROWS]
+    table_ref[...] = whole[:, :split].astype(jnp.bfloat16)
+    rest = whole[:, split:]
+    gas_lane = lax.broadcasted_iota(jnp.int32, rest.shape, 1) < first_row - split
+    mixed_ref[:points] = jnp.where(gas_lane, rest, 0.0).astype(jnp.bfloat16)
+    mixed_ref[points:] = jnp.where(gas_lane, 0.0, rest).astype(jnp.bfloat16)
     for copy in copies[3:]:
         copy.wait()
 
@@ -142,14 +145,14 @@
                 amount = jnp.broadcast_to(block_ref[slot, place : place + 1, :], (PACK, LANES)).astype(jnp.bfloat16)
                 pair.append(jnp.concatenate([amount] * (BIN_ROWS // PACK), axis=0) * selector)
             parts.append(jnp.concatenate(pair, axis=1))
+        parts.append(jnp.concatenate(selectors, axis=1))
         weighted = jnp.concatenate(parts, axis=0)
-        selected = jnp.concatenate(selectors, axis=1)
-        tau = jnp.dot(table_ref[...], weighted, preferred_element_type=jnp.float32)
-        albedo = jnp.dot(scatter_ref[...], selected, preferred_element_type=jnp.float32)
+        tau = jnp.dot(table_ref[...], weighted[:split], preferred_element_type=jnp.float32)
+        mixed = jnp.dot(mixed_ref[...], weighted[split:], preferred_element_type=jnp.float32)
         for near in range(2):
             cols = slice(near * LANES, (near + 1) * LANES)
-            optic_ref[layer + near, :points] = tau[:, cols]
-            optic_ref[layer + near, points:] = albedo[:, cols]
+            optic_ref[layer + near, :points] = tau[:, cols] + mixed[:points, cols]
+            optic_ref[layer + near, points:] = mixed[points:, cols]
 
     def advance(first, part, cosine, slope):
         rows = slice(part * half, (part + 1) * half)
@@ -270,6 +273,7 @@
     field = pltpu.VMEM((levels, points, LANES), jnp.float32)
     state = pltpu.VMEM((points, LANES), jnp.float32)
     rows = gas_count * levels + levels + PACK
+    split = (gas_count + 1) * BIN_ROWS // 2 // LANES * LANES
     blocks = columns // LANES
     heat = pl.pallas_call(
         functools.partial(heating_kernel, columns // group_size),
@@ -287,8 +291,8 @@
             pltpu.VMEM((bins, points), scattering.dtype),
             pltpu.SemaphoreType.DMA((8,)),
             pltpu.VMEM((-(-(gas_count + 1) * BIN_ROWS // LANES) * LANES, LANES), jnp.float32),
-            pltpu.VMEM((points, gas_count * BIN_ROWS), jnp.bfloat16),
-            pltpu.VMEM((points, BIN_ROWS), jnp.bfloat16),
+            pltpu.VMEM((points, split), jnp.bfloat16),
+            pltpu.VMEM((2 * points, (gas_count + 1) * BIN_ROWS - split), jnp.bfloat16),
             pltpu.VMEM((blocks, rows, LANES), jnp.float32),
             pltpu.VMEM((levels, 2 * points, LANES), jnp.float32),
             field,

time: 22.6 us -> 23.3 us (1.031)
  Pallas kernels: 13.7 us -> 14.4 us
    pallas_call x1, Pallas kernels: 12 us -> 12.8 us  [local(): pl.pallas_call(functools.partial(heating_kernel, columns // group_size),...]
  transfers between devices with their start and end apart: 1 -> 1, of which waited for: 0 -> 0; matrix products, arithmetic and copies ran while one was open for 0% -> 0% of each run, Pallas kernels for 54% -> 55%
where the time goes in v2:
time: 23.3 us; the launch traced here: 23.1 us
  Pallas kernels  14.4 us (62%)
  starting transfers between devices  7.28 us (31%)
  local copies, waits for them, and re-layouts  1.4 us (6%)
    pallas_call x1, Pallas kernels, local(): pl.pallas_call(functools.partial(heating_kernel, columns // group_size),...  12.8 us
    all_to_all x1, starting transfers between devices, local(): lax.all_to_all(wanted, 'span', split_axis=0, concat_axis=0, tiled=True)  7.28 us
    pallas_call x1, Pallas kernels, local(): pl.pallas_call(shade_kernel, out_shape=jax.ShapeDtypeStruct((levels, colu...  1.61 us
    broadcast_in_dim x1, local copies, waits for them, and re-layouts, local(): jnp.broadcast_to(sunlit[:, None], (block_count, group_size // block_count))  0.72 us
    reshape x1, local copies, waits for them, and re-layouts, local(): jnp.broadcast_to(sunlit[:, None], (block_count, group_size // block_count))  0.68 us
  transfers between devices with their start and end apart: 1, of which 0 were waited for; matrix products, arithmetic and copies ran while one was open for 0% of the time, Pallas kernels for 55%

profile of v2, /device:TPU:0, one launch (start us, length us, event | category | flops | bytes accessed | tf_op | source)
XLA Modules:
  0.0 23.1 jit_solution(12307791918132942178)
XLA Ops:
  0.0 0.7 %broadcast_in_dim.2 = s32[4,2]{1,0:T(4,128)S(1)} broadcast(s32[4]{0:T(128)} %param.15), dimensions={0} | broadcast | bytes 48 | tf_op jit(solution)/shard_map/broadcast_in_dim | solution.py:271
  0.7 0.7 %reshape.9 = s32[8,1,1]{2,1,0:T(1,128)} reshape(s32[4,2]{1,0:T(4,128)S(1)} %broadcast_in_dim.2) | data formatting | bytes 64 | tf_op jit(solution)/shard_map/reshape | solution.py:271
  1.4 7.3 %all-to-all-start = ((s32[8,1,1]{2,1,0:T(1,128)}), s32[8,1,1]{2,1,0:T(1,128)S(1)}, u32[]{:S(2)}, u32[]{:S(2)}) async-start(s32[8,1,1]{2,1,0:T(1,128)} %reshape.9), calls=%async_computation | async-start | bytes 8192 | tf_op jit(solution)/shard_map/all_to_all | solution.py:272
  8.7 12.8 %shard_map.91.heat_hbm = f32[40,512]{1,0:T(8,128)} custom-call(bf16[7,32,512]{2,1,0:T(8,128)(2,1)} %gases_hbm.1, s32[32,512]{1,0:T(8,128)} %bins_hbm.1, bf16[32,512]{1,0:T(8,128)(2,1)} %mass_hbm.1, bf16[512]{0:T(512)(128)(2,1)} %cosine_hbm.1, bf16[512]{0:T(512)(128)(2,1)} %ground_hbm.1, s32[1,512]{1,0:T(1,128)} %bitcast.5, bf16[7,60,112]{2,1,0:T(8,128)(2,1)} %bitcast.3, ...), custom_call_target="tpu_custom_call" | custom-call | flops 73400320 | bytes 1048576 | tf_op jit(solution)/shard_map/pallas_call | solution.py:278
  21.5 0.0 all-to-all-done.flags_ref
  21.5 1.6 %shard_map.92 = f32[32,512]{1,0:T(8,128)} custom-call(f32[40,512]{1,0:T(8,128)} %shard_map.91.heat_hbm, s32[8,1,1]{2,1,0:T(1,128)S(1)} %all-to-all-done.flags_ref), custom_call_target="tpu_custom_call" | custom-call | tf_op jit(solution)/shard_map/pallas_call | solution.py:322
Async XLA Ops:
  1.4 20.1 %all-to-all-start = ((s32[8,1,1]{2,1,0:T(1,128)}), s32[8,1,1]{2,1,0:T(1,128)S(1)}, u32[]{:S(2)}, u32[]{:S(2)}) async-start(s32[8,1,1]{2,1,0:T(1,128)} %reshape.9), calls=%async_computation | async-start | bytes 8192 | tf_op jit(solution)/shard_map/all_to_all | solution.py:272

commit v3 on v1

--- a/solution.py
+++ b/solution.py
@@ -12,7 +12,7 @@
 ROWS = 8
 PACK = 16
 STEP = 8
-HALVES = 2
+PARTS = 4
 BIN_ROWS = 64
 LOG2E = math.log2(math.e)
 VMEM_BYTES = 63 * 1024 * 1024
@@ -61,8 +61,7 @@
     gas_count, levels, columns = gases_ref.shape
     points = table_ref.shape[0]
     bin_count = absorb_ref.shape[1]
-    half = points // HALVES
-    vregs = half // ROWS
+    edges = [part * (points // ROWS) // PARTS * ROWS for part in range(PARTS + 1)]
     blocks = columns // LANES
     bin_row = gas_count * levels
     ray_row = bin_row + levels
@@ -152,9 +151,10 @@
             optic_ref[layer + near, points:] = albedo[:, cols]
 
     def advance(first, part, cosine, slope):
-        rows = slice(part * half, (part + 1) * half)
-        half_rows = slice(points + part * half, points + (part + 1) * half)
-        shape = (vregs, ROWS, LANES)
+        rows = slice(edges[part], edges[part + 1])
+        half_rows = slice(points + edges[part], points + edges[part + 1])
+        size = edges[part + 1] - edges[part]
+        shape = (size // ROWS, ROWS, LANES)
         if first > 0:
             refl = refl_buf[rows].reshape(shape)
             fall = fall_buf[rows].reshape(shape)
@@ -171,36 +171,36 @@
             below = direct * passed
             source = half_albedo * (direct - below)
             if layer == 0:
-                up_buf[layer, rows] = transmit.reshape(half, LANES)
-                rise_buf[layer, rows] = source.reshape(half, LANES)
+                up_buf[layer, rows] = transmit.reshape(size, LANES)
+                rise_buf[layer, rows] = source.reshape(size, LANES)
                 fall = source
                 refl = reflect
             else:
-                pass_buf[layer, rows] = (1.0 - refl).reshape(half, LANES)
+                pass_buf[layer, rows] = (1.0 - refl).reshape(size, LANES)
                 inverse = pl.reciprocal(1.0 - reflect * refl, approx=True)
                 up = transmit * inverse
                 rise = (reflect * fall + source) * inverse
-                up_buf[layer, rows] = up.reshape(half, LANES)
-                rise_buf[layer, rows] = rise.reshape(half, LANES)
+                up_buf[layer, rows] = up.reshape(size, LANES)
+                rise_buf[layer, rows] = rise.reshape(size, LANES)
                 fall = source + transmit * (fall + refl * rise)
                 refl = reflect + transmit * (refl * up)
             direct = below
             gain_buf[part, layer + 1] = jnp.sum(direct + fall, axis=0)
-        refl_buf[rows] = refl.reshape(half, LANES)
-        fall_buf[rows] = fall.reshape(half, LANES)
-        direct_buf[rows] = direct.reshape(half, LANES)
+        refl_buf[rows] = refl.reshape(size, LANES)
+        fall_buf[rows] = fall.reshape(size, LANES)
+        direct_buf[rows] = direct.reshape(size, LANES)
 
     lead = range(0, STEP, 2)
 
     def column_block(block, carry):
         cosine = block_ref[block, ray_row : ray_row + ROWS]
         slope = (-LOG2E) / cosine
-        for part in range(HALVES):
-            gain_buf[part, 0] = cosine * float(vregs)
+        for part in range(PARTS):
+            gain_buf[part, 0] = cosine * float((edges[part + 1] - edges[part]) // ROWS)
         for first in range(0, levels, STEP):
             coming = [layer for layer in range(first + STEP, first + 2 * STEP, 2) if layer < levels]
-            for part in range(HALVES):
-                for layer in coming[part * len(coming) // HALVES : (part + 1) * len(coming) // HALVES]:
+            for part in range(PARTS):
+                for layer in coming[part * len(coming) // PARTS : (part + 1) * len(coming) // PARTS]:
                     optical(block, layer)
                 advance(first, part, cosine, slope)
 
@@ -216,7 +216,7 @@
 
         def total(level):
             summed = gain_buf[0, level]
-            for part in range(1, HALVES):
+            for part in range(1, PARTS):
                 summed = summed + gain_buf[part, level]
             return summed
 
@@ -297,7 +297,7 @@
             state,
             state,
             state,
-            pltpu.VMEM((HALVES, levels + 1, ROWS, LANES), jnp.float32),
+            pltpu.VMEM((PARTS, levels + 1, ROWS, LANES), jnp.float32),
             pltpu.VMEM((levels + 1, ROWS, LANES), jnp.float32),
             pltpu.VMEM((blocks, levels, LANES), jnp.float32),
         ],

time: 22.6 us -> 22.7 us (level)
  no operation moved by 1% of the time
where the time goes in v3:
time: 22.7 us; the launch traced here: 22.5 us
  Pallas kernels  13.8 us (61%)
  starting transfers between devices  7.28 us (32%)
  local copies, waits for them, and re-layouts  1.4 us (6%)
    pallas_call x1, Pallas kernels, local(): pl.pallas_call(functools.partial(heating_kernel, columns // group_size),...  12.1 us
    all_to_all x1, starting transfers between devices, local(): lax.all_to_all(wanted, 'span', split_axis=0, concat_axis=0, tiled=True)  7.28 us
    pallas_call x1, Pallas kernels, local(): pl.pallas_call(shade_kernel, out_shape=jax.ShapeDtypeStruct((levels, colu...  1.61 us
    broadcast_in_dim x1, local copies, waits for them, and re-layouts, local(): jnp.broadcast_to(sunlit[:, None], (block_count, group_size // block_count))  0.72 us
    reshape x1, local copies, waits for them, and re-layouts, local(): jnp.broadcast_to(sunlit[:, None], (block_count, group_size // block_count))  0.68 us
  transfers between devices with their start and end apart: 1, of which 0 were waited for; matrix products, arithmetic and copies ran while one was open for 0% of the time, Pallas kernels for 54%

profile of v3, /device:TPU:0, one launch (start us, length us, event | category | flops | bytes accessed | tf_op | source)
XLA Modules:
  0.0 22.5 jit_solution(5441495126258597821)
XLA Ops:
  0.0 0.7 %broadcast_in_dim.2 = s32[4,2]{1,0:T(4,128)S(1)} broadcast(s32[4]{0:T(128)} %param.15), dimensions={0} | broadcast | bytes 48 | tf_op jit(solution)/shard_map/broadcast_in_dim | solution.py:268
  0.7 0.7 %reshape.9 = s32[8,1,1]{2,1,0:T(1,128)} reshape(s32[4,2]{1,0:T(4,128)S(1)} %broadcast_in_dim.2) | data formatting | bytes 64 | tf_op jit(solution)/shard_map/reshape | solution.py:268
  1.4 7.3 %all-to-all-start = ((s32[8,1,1]{2,1,0:T(1,128)}), s32[8,1,1]{2,1,0:T(1,128)S(1)}, u32[]{:S(2)}, u32[]{:S(2)}) async-start(s32[8,1,1]{2,1,0:T(1,128)} %reshape.9), calls=%async_computation | async-start | bytes 8192 | tf_op jit(solution)/shard_map/all_to_all | solution.py:269
  8.7 12.1 %shard_map.91.heat_hbm = f32[40,512]{1,0:T(8,128)} custom-call(bf16[7,32,512]{2,1,0:T(8,128)(2,1)} %gases_hbm.1, s32[32,512]{1,0:T(8,128)} %bins_hbm.1, bf16[32,512]{1,0:T(8,128)(2,1)} %mass_hbm.1, bf16[512]{0:T(512)(128)(2,1)} %cosine_hbm.1, bf16[512]{0:T(512)(128)(2,1)} %ground_hbm.1, s32[1,512]{1,0:T(1,128)} %bitcast.5, bf16[7,60,112]{2,1,0:T(8,128)(2,1)} %bitcast.3, ...), custom_call_target="tpu_custom_call" | custom-call | flops 73400320 | bytes 1048576 | tf_op jit(solution)/shard_map/pallas_call | solution.py:274
  20.8 0.0 all-to-all-done.flags_ref
  20.8 1.6 %shard_map.92 = f32[32,512]{1,0:T(8,128)} custom-call(f32[40,512]{1,0:T(8,128)} %shard_map.91.heat_hbm, s32[8,1,1]{2,1,0:T(1,128)S(1)} %all-to-all-done.flags_ref), custom_call_target="tpu_custom_call" | custom-call | tf_op jit(solution)/shard_map/pallas_call | solution.py:318
Async XLA Ops:
  1.4 19.4 %all-to-all-start = ((s32[8,1,1]{2,1,0:T(1,128)}), s32[8,1,1]{2,1,0:T(1,128)S(1)}, u32[]{:S(2)}, u32[]{:S(2)}) async-start(s32[8,1,1]{2,1,0:T(1,128)} %reshape.9), calls=%async_computation | async-start | bytes 8192 | tf_op jit(solution)/shard_map/all_to_all | solution.py:269
